TPU v7x, 128 devices: a whole 4x4x4 slice. The times are simulated.
128 devices in a mesh: ctx: 16 (over x_hi, y, core), tp: 8 (over z, x_lo).
Axes of the slice: x: 4 (x_hi: 2, x_lo: 2; x = x_hi * 2 + x_lo), y: 4, z: 4, core: 2. Of those that a mesh axis runs over, the one named last changes fastest.
Arguments:
- activations: bfloat16 [1536, 8, 4096], P('ctx'), may hold values from -100 to 100
- w_query: bfloat16 [4096, 4096], P(None, 'tp'), may hold values from -0.09375 to 0.09375
- w_key: bfloat16 [4096, 4096], P(None, 'tp'), may hold values from -0.09375 to 0.09375
- w_value: bfloat16 [4096, 4096], P(None, 'tp'), may hold values from -0.09375 to 0.09375
- pre_mix: float32 [32, 32], replicated, may hold values from -1 to 1
- post_mix: float32 [32, 32], replicated, may hold values from -1 to 1
- span_place: int32 [32], replicated, may hold values from 0 to 31, each once
Outputs:
- attended: bfloat16 [1536, 8, 4096], P('ctx', 'tp')
Inputs may be any that keep to these rules, and one draw needn't show every extreme that they name: `span_place`: every stored span slot holds a different span of the sequence.
All inputs are finite; a program needn't handle non-finite values.
Results may differ from a plain program's by a relative error of at most 0.012.
The roundings to bfloat16 on the way count: a program that leaves them out, or rounds other values in their place, can miss the bound.
Values may be sent and summed in bfloat16 or wider, within the bound.
A program may use at most 192 MiB of HBM per device.

v0:
```python
import functools

import jax
import jax.numpy as jnp
from jax import lax
from jax.experimental import pallas as pl
from jax.experimental.pallas import tpu as pltpu
from jax.sharding import PartitionSpec as P

HEADS = 32
HD = 128
SPAN = 48
MODEL = 4096
SEQS = 8
ROWS = 96
TILE = 384
SLAB = 8
SLABS = TILE // SLAB
MIX = HEADS * SLAB
WIDE = 256
HALF = 2048
FLOOR = -1e30
MESH = pl.DeviceIdType.MESH
F32 = jnp.float32
BF16 = jnp.bfloat16

CHUNKS = ((1, 0), (0, 0), (1, 1), (0, 1), (2, 0), (2, 1))


def dot(a, b):
    return jnp.dot(a, b, preferred_element_type=F32)


def split(x):
    high = x.astype(BF16)
    return high, (x - high.astype(F32)).astype(BF16)


def spread_mix(mix, high_ref, low_ref):
    row = lax.broadcasted_iota(jnp.int32, (MIX, HEADS), 0) // SLAB
    col = lax.broadcasted_iota(jnp.int32, (MIX, HEADS), 1)
    pick = jnp.where(row == col, 1.0, 0.0).astype(BF16)
    same = (lax.broadcasted_iota(jnp.int32, (MIX, MIX), 0) % SLAB) == (
        lax.broadcasted_iota(jnp.int32, (MIX, MIX), 1) % SLAB
    )
    for part, ref in zip(split(mix), (high_ref, low_ref)):
        tall = dot(pick, part).astype(BF16)
        full = lax.dot_general(tall, pick, (((1,), (1,)), ((), ())), preferred_element_type=F32)
        ref[...] = jnp.where(same, full, 0.0).astype(BF16)


def kernel(
    act, w_query, w_key, w_value, pre_mix, post_mix, query_pos, key_pos, out,
    act_v, w_v, res, stage, q_buf, k_buf, v_buf, scores, stat, stat_in,
    part, part_in, pre_high, pre_low, post_high, post_low,
    act_sem, w_sem, own_sem, a2a_send, a2a_recv, y_send, y_recv, q_send, q_recv,
    stat_send, stat_recv, p_send, p_recv,
):
    ctx, tp = lax.axis_index("ctx"), lax.axis_index("tp")
    xh, y, core = ctx // 8, (ctx // 2) % 4, ctx % 2
    up = (xh * 8 + ((y + 1) % 4) * 2 + core, tp)
    down = (xh * 8 + ((y + 3) % 4) * 2 + core, tp)
    y_up, y_down = (y + 1) % 4, (y + 3) % 4
    sibling = (ctx + 1 - 2 * core, tp)
    partner = ((1 - xh) * 8 + y * 2 + core, tp)
    diagonal = ((1 - xh) * 8 + y * 2 + 1 - core, tp)
    mine = xh * 2 + core
    sibling_slot = xh * 2 + 1 - core
    partner_slot = (1 - xh) * 2 + core
    diagonal_slot = (1 - xh) * 2 + 1 - core
    peers = [(ctx, (tp + o) % SEQS) for o in range(1, SEQS)]

    weights = (w_query, w_key, w_value)
    buffers = (q_buf, k_buf, v_buf)

    act_copies = []
    for b in range(3):
        rows = pl.ds(b * 32, 32)
        act_copies.append(pltpu.make_async_copy(act.at[rows], act_v.at[rows], act_sem.at[b]))
    w_copies = []
    for n, (kind, j) in enumerate(CHUNKS):
        w_copies.append(
            pltpu.make_async_copy(weights[kind].at[:, pl.ds(j * WIDE, WIDE)], w_v.at[n], w_sem.at[n])
        )
    w_copies[0].start()
    for c in act_copies:
        c.start()
    for c in w_copies[1:]:
        c.start()

    barrier = pltpu.get_barrier_semaphore()
    friends = peers + [up, down, sibling, partner, diagonal]
    for friend in friends:
        pl.semaphore_signal(barrier, inc=1, device_id=friend, device_id_type=MESH)
    pl.semaphore_wait(barrier, len(friends))

    sends = []

    def remote(src, dst, send, recv, to):
        copy = pltpu.make_async_remote_copy(
            src_ref=src, dst_ref=dst, send_sem=send, recv_sem=recv, device_id=to, device_id_type=MESH
        )
        sends.append(copy)
        return copy

    def slot_of(kind):
        return mine if kind == 0 else y

    exchange = {}

    def project(n):
        kind, j = CHUNKS[n]
        w_copies[n].wait()
        for b in range(3):
            if n == 0:
                act_copies[b].wait()
            rows = act_v[b * 32:(b + 1) * 32].reshape(32 * SEQS, MODEL)
            both = dot(rows, w_v[n])
            for i in range(2):
                res[i] = both[:, i * HD:(i + 1) * HD]
            for s in range(SEQS):
                for i in range(2):
                    stage[n, s, b * 32:(b + 1) * 32, i * HD:(i + 1) * HD] = res[
                        i, pl.ds(s, 32, stride=SEQS), :
                    ].astype(BF16)
        here = buffers[kind].at[j, slot_of(kind), :, pl.ds(pl.multiple_of(tp * WIDE, WIDE), WIDE)]
        copies = []
        for o, peer in enumerate(peers):
            copies.append(
                remote(stage.at[n, peer[1]], here, a2a_send.at[n, o], a2a_recv.at[n, o], peer)
            )
            copies[-1].start()
        own = pltpu.make_async_copy(stage.at[n, tp], here, own_sem.at[n])
        own.start()
        exchange[n] = (copies, own)

    def arrived(n):
        copies, own = exchange[n]
        own.wait()
        for c in copies:
            c.wait_recv()

    ring = {}

    def ring_start(n, r):
        kind, j = CHUNKS[n]
        buf = buffers[kind]
        arrived(n)
        a = remote(buf.at[j, y], buf.at[j, y], y_send.at[r, 0], y_recv.at[r, 0], up)
        b = remote(buf.at[j, y], buf.at[j, y], y_send.at[r, 1], y_recv.at[r, 1], down)
        a.start()
        b.start()
        ring[r] = [a, b]

    def ring_forward(n, r):
        kind, j = CHUNKS[n]
        buf = buffers[kind]
        a, b = ring[r]
        a.wait_recv()
        first = buf.at[j, y_down, pl.ds(0, 48)]
        c = remote(first, first, y_send.at[r, 2], y_recv.at[r, 2], up)
        c.start()
        b.wait_recv()
        second = buf.at[j, y_up, pl.ds(48, 48)]
        d = remote(second, second, y_send.at[r, 3], y_recv.at[r, 3], down)
        d.start()
        ring[r] = [c, d]

    def ring_finish(r):
        for c in ring[r]:
            c.wait_recv()

    queries = {}

    def query_start(n):
        _, j = CHUNKS[n]
        arrived(n)
        a = remote(q_buf.at[j, mine], q_buf.at[j, mine], q_send.at[j, 1], q_recv.at[j, 1], partner)
        b = remote(q_buf.at[j, mine], q_buf.at[j, mine], q_send.at[j, 0], q_recv.at[j, 0], sibling)
        a.start()
        b.start()
        queries[j] = [a, b]

    def query_forward(j):
        a, b = queries[j]
        a.wait_recv()
        there = q_buf.at[j, partner_slot]
        c = remote(there, there, q_send.at[j, 2], q_recv.at[j, 2], sibling)
        c.start()
        queries[j] = [b, c]

    def query_finish(j):
        for c in queries[j]:
            c.wait_recv()

    def score(j):
        def one(hh, carry):
            lanes = pl.ds(pl.multiple_of(hh * HD, HD), HD)
            q = q_buf[j, :, :, lanes].reshape(TILE, HD)
            k = k_buf[j, :, :, lanes].reshape(TILE, HD)
            scores[(hh // 2) * 4 + 2 * j + hh % 2] = lax.dot_general(
                q, k, (((1,), (1,)), ((), ())), preferred_element_type=F32
            )
            return carry

        lax.fori_loop(0, HEADS // 2, one, 0)

    lane = lax.broadcasted_iota(jnp.int32, (MIX, 128), 1)

    def softmax(first, last):
        def one(i, carry):
            rows = pl.ds(pl.multiple_of(i * SLAB, SLAB), SLAB)
            x = scores[:, rows, :].reshape(MIX, TILE)
            high, low = split(x)
            logits = dot(pre_high[...], high) + dot(pre_low[...], high) + dot(pre_high[...], low)
            seen = key_pos[...] <= query_pos[rows, :]
            masked = jnp.where(seen[None], logits.reshape(HEADS, SLAB, TILE), FLOOR).reshape(MIX, TILE)
            top = jnp.max(masked, axis=1, keepdims=True)
            e = jnp.exp(masked - top)
            total = jnp.sum(e, axis=1, keepdims=True)
            scores[:, rows, :] = e.reshape(HEADS, SLAB, TILE)
            stat[...] = jnp.where(lane == i, top, jnp.where(lane == i + 64, total, stat[...]))
            return carry

        lax.fori_loop(first, last, one, 0)

    def post(first, last):
        def one(i, carry):
            rows = pl.ds(pl.multiple_of(i * SLAB, SLAB), SLAB)
            weight = jnp.sum(jnp.where(lane == i, stat[...], 0.0), axis=1, keepdims=True)
            probs = (scores[:, rows, :].reshape(MIX, TILE) * weight).astype(BF16)
            mixed = dot(post_high[...], probs) + dot(post_low[...], probs)
            scores[:, rows, :] = mixed.reshape(HEADS, SLAB, TILE)
            return carry

        lax.fori_loop(first, last, one, 0)

    def attend(j):
        def one(hh, carry):
            lanes = pl.ds(pl.multiple_of(hh * HD, HD), HD)
            v = v_buf[j, :, :, lanes].reshape(TILE, HD)
            m = scores[(hh // 2) * 4 + 2 * j + hh % 2].astype(BF16)
            part[j, :, :, lanes] = dot(m, v).reshape(4, ROWS, HD).astype(BF16)
            return carry

        lax.fori_loop(0, HEADS // 2, one, 0)

    partial = {}

    def partial_start(j):
        a = remote(part.at[j, diagonal_slot], part_in.at[j, 0], p_send.at[j, 0], p_recv.at[j, 0], sibling)
        b = remote(part.at[j, sibling_slot], part_in.at[j, 1], p_send.at[j, 1], p_recv.at[j, 1], sibling)
        a.start()
        b.start()
        partial[j] = [a, b]

    def partial_cross(j):
        a, b = partial[j]
        a.wait_recv()
        part[j, partner_slot] = (
            part[j, partner_slot].astype(F32) + part_in[j, 0].astype(F32)
        ).astype(BF16)
        c = remote(part.at[j, partner_slot], part_in.at[j, 2], p_send.at[j, 2], p_recv.at[j, 2], partner)
        c.start()
        partial[j] = [b, c]

    def partial_finish(j):
        for c in partial[j]:
            c.wait_recv()
        done = (
            part[j, mine].astype(F32) + part_in[j, 1].astype(F32) + part_in[j, 2].astype(F32)
        ).astype(BF16)
        for t in range(SEQS):
            out[:, t * 2 * WIDE + j * WIDE:t * 2 * WIDE + (j + 1) * WIDE] = done[:, t * WIDE:(t + 1) * WIDE]

    project(0)
    project(1)
    project(2)
    ring_start(0, 0)
    project(3)
    project(4)
    query_start(1)
    project(5)
    spread_mix(pre_mix[...] * (HD ** -0.5), pre_high, pre_low)
    spread_mix(post_mix[...], post_high, post_low)
    stat[...] = jnp.zeros_like(stat)
    ring_start(2, 1)
    ring_forward(0, 0)
    query_start(3)
    query_forward(0)
    ring_start(4, 2)
    ring_finish(0)
    query_finish(0)
    score(0)
    ring_forward(2, 1)
    query_forward(1)
    ring_start(5, 3)
    ring_finish(1)
    query_finish(1)
    score(1)
    softmax(0, 24)
    ring_forward(4, 2)
    softmax(24, 48)
    ring_forward(5, 3)
    stat_copies = []
    for n, to in enumerate((sibling, partner, diagonal)):
        stat_copies.append(remote(stat, stat_in.at[n], stat_send.at[n], stat_recv.at[n], to))
        stat_copies[-1].start()
    for c in stat_copies:
        c.wait_recv()
    for c in stat_copies:
        c.wait_send()
    del sends[-3:]
    own = stat[...]
    others = [stat_in[n] for n in range(3)]
    top = functools.reduce(jnp.maximum, others, own)
    total = sum(jnp.exp(s - top) * pltpu.roll(s, 64, 1) for s in [own] + others)
    stat[...] = jnp.exp(own - top) / total
    post(0, 48)
    ring_finish(2)
    attend(0)
    partial_start(0)
    ring_finish(3)
    partial_cross(0)
    attend(1)
    partial_start(1)
    partial_cross(1)
    partial_finish(0)
    partial_finish(1)
    for c in sends:
        c.wait_send()


def local(activations, w_query, w_key, w_value, pre_mix, post_mix, span_place):
    ctx = lax.axis_index("ctx")
    xh, y, core = ctx // 8, (ctx // 2) % 4, ctx % 2
    positions = (span_place[:, None] * SPAN + jnp.arange(SPAN, dtype=jnp.int32)[None, :]).reshape(2, 4, 2, ROWS)
    query_pos = lax.dynamic_index_in_dim(positions, y, 1, keepdims=False).reshape(TILE, 1)
    key_pos = lax.dynamic_index_in_dim(positions, xh, 0, keepdims=False)
    key_pos = lax.dynamic_index_in_dim(key_pos, core, 1, keepdims=False).reshape(1, TILE)
    any_spec = pl.BlockSpec(memory_space=pl.ANY)
    vmem = pl.BlockSpec(memory_space=pltpu.VMEM)
    dma = pltpu.SemaphoreType.DMA
    out = pl.pallas_call(
        kernel,
        name="heads",
        out_shape=jax.ShapeDtypeStruct((ROWS, MODEL), BF16),
        in_specs=[any_spec] * 4 + [vmem] * 4,
        out_specs=vmem,
        scratch_shapes=[
            pltpu.VMEM((ROWS, SEQS, MODEL), BF16),
            pltpu.VMEM((6, MODEL, WIDE), BF16),
            pltpu.VMEM((2, 256, HD), F32),
            pltpu.VMEM((6, SEQS, ROWS, WIDE), BF16),
            pltpu.VMEM((2, 4, ROWS, HALF), BF16),
            pltpu.VMEM((2, 4, ROWS, HALF), BF16),
            pltpu.VMEM((2, 4, ROWS, HALF), BF16),
            pltpu.VMEM((HEADS, TILE, TILE), F32),
            pltpu.VMEM((MIX, 128), F32),
            pltpu.VMEM((3, MIX, 128), F32),
            pltpu.VMEM((2, 4, ROWS, HALF), BF16),
            pltpu.VMEM((2, 3, ROWS, HALF), BF16),
            pltpu.VMEM((MIX, MIX), BF16),
            pltpu.VMEM((MIX, MIX), BF16),
            pltpu.VMEM((MIX, MIX), BF16),
            pltpu.VMEM((MIX, MIX), BF16),
            dma((3,)), dma((6,)), dma((6,)),
            dma((6, 7)), dma((6, 7)),
            dma((4, 4)), dma((4, 4)),
            dma((2, 3)), dma((2, 3)),
            dma((3,)), dma((3,)),
            dma((2, 3)), dma((2, 3)),
        ],
        compiler_params=pltpu.CompilerParams(
            collective_id=0, has_side_effects=True, vmem_limit_bytes=60 * 2**20
        ),
        cost_estimate=pl.CostEstimate(flops=30 * 10**9, bytes_accessed=30 * 10**6, transcendentals=5 * 10**6),
    )(activations, w_query, w_key, w_value, pre_mix, post_mix, query_pos, key_pos)
    return out.reshape(ROWS, 1, MODEL)


def solution(mesh):
    placed = (P("ctx", None, None), P(None, "tp"), P(None, "tp"), P(None, "tp"), P(), P(), P())
    return jax.shard_map(
        local, mesh=mesh, in_specs=placed, out_specs=P("ctx", "tp", None), check_vma=False
    )
```

profile of v0, /device:TPU:1, one launch (start us, length us, event | category | flops | bytes accessed | tf_op | source)
XLA Modules:
  0.0 146.6 jit_solution(15066056190117007271)
XLA Ops:
  0.0 0.7 broadcast_multiply_fusion
  0.7 0.1 add.51
  0.7 0.1 add.47
  0.9 0.1 add.48
  0.9 0.1 add.49
  1.1 0.7 reshape.21.key_pos
  1.7 0.8 reshape.23.query_pos
  2.6 141.9 %heads.1 = bf16[96,4096]{1,0:T(8,128)(2,1)} custom-call(bf16[96,8,4096]{2,1,0:T(8,128)(2,1)} %act.1, bf16[4096,512]{1,0:T(8,128)(2,1)} %w_query.1, bf16[4096,512]{1,0:T(8,128)(2,1)} %w_key.1, bf16[4096,512]{1,0:T(8,128)(2,1)} %w_value.1, f32[32,32]{1,0:T(8,128)} %pre_mix.1, f32[32,32]{1,0:T(8,128)} %post_mix.1, s32[384,1]{1,0:T(8,128)} %reshape.23.query_pos, ...), custom_call_target="tpu_custom_call" | custom-call | flops 30000001024 | bytes 30000000 | tf_op jit(solution)/shard_map/heads/pallas_call | solution.py:344
  144.5 2.1 %copy.12 = bf16[96,1,4096]{2,0,1:T(8,128)(2,1)} copy(bf16[96,1,4096]{2,0,1:T(8,128)(2,1)} %bitcast.5) | data formatting | bytes 1572864
  (5 shorter events, 0.1 us)
where the time goes:
time: 147 us
  Pallas kernels  142 us (97%)
  local copies, waits for them, and re-layouts  3.96 us (3%)
    pallas_call x1, Pallas kernels, local(): pl.pallas_call(kernel, name='heads', out_shape=jax.ShapeDtypeStruct((ROWS...  142 us

commit v1 on v0

--- a/solution.py
+++ b/solution.py
@@ -50,8 +50,8 @@
 
 
 def kernel(
-    act, w_query, w_key, w_value, pre_mix, post_mix, query_pos, key_pos, out,
-    act_v, w_v, res, stage, q_buf, k_buf, v_buf, scores, stat, stat_in,
+    act, w_query, w_key, w_value, pre_mix, post_mix, span_place, out,
+    act_v, w_v, res, stage, q_buf, k_buf, v_buf, scores, stat, stat_in, key_pos,
     part, part_in, pre_high, pre_low, post_high, post_low,
     act_sem, w_sem, own_sem, a2a_send, a2a_recv, y_send, y_recv, q_send, q_recv,
     stat_send, stat_recv, p_send, p_recv,
@@ -85,14 +85,21 @@
     w_copies[0].start()
     for c in act_copies:
         c.start()
-    for c in w_copies[1:]:
-        c.start()
 
     barrier = pltpu.get_barrier_semaphore()
     friends = peers + [up, down, sibling, partner, diagonal]
     for friend in friends:
         pl.semaphore_signal(barrier, inc=1, device_id=friend, device_id_type=MESH)
-    pl.semaphore_wait(barrier, len(friends))
+
+    spread_mix(pre_mix[...] * (HD ** -0.5), pre_high, pre_low)
+    spread_mix(post_mix[...], post_high, post_low)
+    stat[...] = jnp.zeros_like(stat)
+    column = lax.broadcasted_iota(jnp.int32, (SLAB, TILE), 1)
+    position = column % SPAN
+    for n in range(TILE // SPAN):
+        place = span_place[(xh * 8 + (n // 2) * 2 + core) * 2 + n % 2]
+        position = jnp.where(column // SPAN == n, position + place * SPAN, position)
+    key_pos[...] = position
 
     sends = []
 
@@ -114,6 +121,9 @@
         for b in range(3):
             if n == 0:
                 act_copies[b].wait()
+                if b == 2:
+                    w_copies[1].start()
+                    w_copies[2].start()
             rows = act_v[b * 32:(b + 1) * 32].reshape(32 * SEQS, MODEL)
             both = dot(rows, w_v[n])
             for i in range(2):
@@ -123,6 +133,10 @@
                     stage[n, s, b * 32:(b + 1) * 32, i * HD:(i + 1) * HD] = res[
                         i, pl.ds(s, 32, stride=SEQS), :
                     ].astype(BF16)
+        if n == 0:
+            pl.semaphore_wait(barrier, len(friends))
+        elif n + 2 < len(CHUNKS):
+            w_copies[n + 2].start()
         here = buffers[kind].at[j, slot_of(kind), :, pl.ds(pl.multiple_of(tp * WIDE, WIDE), WIDE)]
         copies = []
         for o, peer in enumerate(peers):
@@ -194,79 +208,133 @@
             c.wait_recv()
 
     def score(j):
-        def one(hh, carry):
-            lanes = pl.ds(pl.multiple_of(hh * HD, HD), HD)
-            q = q_buf[j, :, :, lanes].reshape(TILE, HD)
-            k = k_buf[j, :, :, lanes].reshape(TILE, HD)
-            scores[(hh // 2) * 4 + 2 * j + hh % 2] = lax.dot_general(
-                q, k, (((1,), (1,)), ((), ())), preferred_element_type=F32
-            )
+        def one(g, carry):
+            for u in range(4):
+                hh = g * 4 + u
+                lanes = pl.ds(pl.multiple_of(hh * HD, HD), HD)
+                q = q_buf[j, :, :, lanes].reshape(TILE, HD)
+                k = k_buf[j, :, :, lanes].reshape(TILE, HD)
+                scores[(hh // 2) * 4 + 2 * j + hh % 2] = lax.dot_general(
+                    q, k, (((1,), (1,)), ((), ())), preferred_element_type=F32
+                )
             return carry
 
-        lax.fori_loop(0, HEADS // 2, one, 0)
+        lax.fori_loop(0, HEADS // 8, one, 0)
 
     lane = lax.broadcasted_iota(jnp.int32, (MIX, 128), 1)
-
-    def softmax(first, last):
-        def one(i, carry):
-            rows = pl.ds(pl.multiple_of(i * SLAB, SLAB), SLAB)
-            x = scores[:, rows, :].reshape(MIX, TILE)
+    minor = lax.broadcasted_iota(jnp.int32, (SLAB, 1), 0)
+    half = (1 - xh, xh)
+    GROUP = SLABS // 2
+
+    def softmax(group):
+        def one(g, carry):
+            slabs = [g * 4 + u for u in range(4)]
+            rows = [
+                pl.ds(pl.multiple_of((half[group] * GROUP + i) * SLAB, SLAB), SLAB) for i in slabs
+            ]
+            x = jnp.concatenate([scores[:, r, :].reshape(MIX, TILE) for r in rows], axis=1)
             high, low = split(x)
             logits = dot(pre_high[...], high) + dot(pre_low[...], high) + dot(pre_high[...], low)
-            seen = key_pos[...] <= query_pos[rows, :]
-            masked = jnp.where(seen[None], logits.reshape(HEADS, SLAB, TILE), FLOOR).reshape(MIX, TILE)
-            top = jnp.max(masked, axis=1, keepdims=True)
-            e = jnp.exp(masked - top)
-            total = jnp.sum(e, axis=1, keepdims=True)
-            scores[:, rows, :] = e.reshape(HEADS, SLAB, TILE)
-            stat[...] = jnp.where(lane == i, top, jnp.where(lane == i + 64, total, stat[...]))
+            stats = stat[group]
+            for u, (i, r) in enumerate(zip(slabs, rows)):
+                span = i // 6
+                place = span_place[((half[group] * 8 + y * 2) + span // 2) * 2 + span % 2]
+                seen = key_pos[...] <= place * SPAN + (i % 6) * SLAB + minor
+                mine_logits = logits[:, u * TILE:(u + 1) * TILE].reshape(HEADS, SLAB, TILE)
+                masked = jnp.where(seen[None], mine_logits, FLOOR).reshape(MIX, TILE)
+                top = jnp.max(masked, axis=1, keepdims=True)
+                e = jnp.exp(masked - top)
+                total = jnp.sum(e, axis=1, keepdims=True)
+                scores[:, r, :] = e.reshape(HEADS, SLAB, TILE)
+                stats = jnp.where(lane == i, top, jnp.where(lane == i + 64, total, stats))
+            stat[group] = stats
             return carry
 
-        lax.fori_loop(first, last, one, 0)
-
-    def post(first, last):
-        def one(i, carry):
-            rows = pl.ds(pl.multiple_of(i * SLAB, SLAB), SLAB)
-            weight = jnp.sum(jnp.where(lane == i, stat[...], 0.0), axis=1, keepdims=True)
-            probs = (scores[:, rows, :].reshape(MIX, TILE) * weight).astype(BF16)
+        lax.fori_loop(0, GROUP // 4, one, 0)
+
+    stat_copies = {}
+
+    def stat_start(group):
+        copies = []
+        for n, to in enumerate((sibling, partner, diagonal)):
+            copies.append(
+                remote(
+                    stat.at[group], stat_in.at[half[group], n],
+                    stat_send.at[group, n], stat_recv.at[half[group], n], to,
+                )
+            )
+            copies[-1].start()
+        stat_copies[group] = copies
+
+    def stat_finish(group):
+        for c in stat_copies[group]:
+            c.wait_recv()
+        for c in stat_copies[group]:
+            c.wait_send()
+        for c in stat_copies[group]:
+            sends[:] = [d for d in sends if d is not c]
+        own = stat[group]
+        others = [stat_in[half[group], n] for n in range(3)]
+        top = functools.reduce(jnp.maximum, others, own)
+        total = sum(jnp.exp(s - top) * pltpu.roll(s, 64, 1) for s in [own] + others)
+        stat[group] = jnp.exp(own - top) / total
+
+    def post(group):
+        def one(g, carry):
+            slabs = [g * 6 + u for u in range(6)]
+            rows = [
+                pl.ds(pl.multiple_of((half[group] * GROUP + i) * SLAB, SLAB), SLAB) for i in slabs
+            ]
+            weights = stat[group]
+            probs = []
+            for i, r in zip(slabs, rows):
+                weight = jnp.sum(jnp.where(lane == i, weights, 0.0), axis=1, keepdims=True)
+                probs.append((scores[:, r, :].reshape(MIX, TILE) * weight).astype(BF16))
+            probs = jnp.concatenate(probs, axis=1)
             mixed = dot(post_high[...], probs) + dot(post_low[...], probs)
-            scores[:, rows, :] = mixed.reshape(HEADS, SLAB, TILE)
+            for u, r in enumerate(rows):
+                scores[:, r, :] = mixed[:, u * TILE:(u + 1) * TILE].reshape(HEADS, SLAB, TILE)
             return carry
 
-        lax.fori_loop(first, last, one, 0)
-
-    def attend(j):
-        def one(hh, carry):
-            lanes = pl.ds(pl.multiple_of(hh * HD, HD), HD)
-            v = v_buf[j, :, :, lanes].reshape(TILE, HD)
-            m = scores[(hh // 2) * 4 + 2 * j + hh % 2].astype(BF16)
-            part[j, :, :, lanes] = dot(m, v).reshape(4, ROWS, HD).astype(BF16)
+        lax.fori_loop(0, GROUP // 6, one, 0)
+
+    def attend(j, group):
+        rows = pl.ds(pl.multiple_of(half[group] * 2 * ROWS, 2 * ROWS), 2 * ROWS)
+        slots = pl.ds(half[group] * 2, 2)
+
+        def one(g, carry):
+            for u in range(4):
+                hh = g * 4 + u
+                lanes = pl.ds(pl.multiple_of(hh * HD, HD), HD)
+                v = v_buf[j, :, :, lanes].reshape(TILE, HD)
+                m = scores[(hh // 2) * 4 + 2 * j + hh % 2, rows, :].astype(BF16)
+                part[j, slots, :, lanes] = dot(m, v).reshape(2, ROWS, HD).astype(BF16)
             return carry
 
-        lax.fori_loop(0, HEADS // 2, one, 0)
+        lax.fori_loop(0, HEADS // 8, one, 0)
 
     partial = {}
 
-    def partial_start(j):
-        a = remote(part.at[j, diagonal_slot], part_in.at[j, 0], p_send.at[j, 0], p_recv.at[j, 0], sibling)
-        b = remote(part.at[j, sibling_slot], part_in.at[j, 1], p_send.at[j, 1], p_recv.at[j, 1], sibling)
+    def partial_start(j, group):
+        slot = (diagonal_slot, sibling_slot)[group]
+        a = remote(
+            part.at[j, slot], part_in.at[j, group], p_send.at[j, group], p_recv.at[j, group], sibling
+        )
         a.start()
-        b.start()
-        partial[j] = [a, b]
+        partial[j, group] = a
 
     def partial_cross(j):
-        a, b = partial[j]
-        a.wait_recv()
+        partial[j, 0].wait_recv()
         part[j, partner_slot] = (
             part[j, partner_slot].astype(F32) + part_in[j, 0].astype(F32)
         ).astype(BF16)
         c = remote(part.at[j, partner_slot], part_in.at[j, 2], p_send.at[j, 2], p_recv.at[j, 2], partner)
         c.start()
-        partial[j] = [b, c]
+        partial[j, 2] = c
 
     def partial_finish(j):
-        for c in partial[j]:
-            c.wait_recv()
+        partial[j, 1].wait_recv()
+        partial[j, 2].wait_recv()
         done = (
             part[j, mine].astype(F32) + part_in[j, 1].astype(F32) + part_in[j, 2].astype(F32)
         ).astype(BF16)
@@ -281,9 +349,6 @@
     project(4)
     query_start(1)
     project(5)
-    spread_mix(pre_mix[...] * (HD ** -0.5), pre_high, pre_low)
-    spread_mix(post_mix[...], post_high, post_low)
-    stat[...] = jnp.zeros_like(stat)
     ring_start(2, 1)
     ring_forward(0, 0)
     query_start(3)
@@ -298,33 +363,28 @@
     ring_finish(1)
     query_finish(1)
     score(1)
-    softmax(0, 24)
+    softmax(0)
+    stat_start(0)
     ring_forward(4, 2)
-    softmax(24, 48)
+    softmax(1)
+    stat_start(1)
+    stat_finish(0)
+    post(0)
     ring_forward(5, 3)
-    stat_copies = []
-    for n, to in enumerate((sibling, partner, diagonal)):
-        stat_copies.append(remote(stat, stat_in.at[n], stat_send.at[n], stat_recv.at[n], to))
-        stat_copies[-1].start()
-    for c in stat_copies:
-        c.wait_recv()
-    for c in stat_copies:
-        c.wait_send()
-    del sends[-3:]
-    own = stat[...]
-    others = [stat_in[n] for n in range(3)]
-    top = functools.reduce(jnp.maximum, others, own)
-    total = sum(jnp.exp(s - top) * pltpu.roll(s, 64, 1) for s in [own] + others)
-    stat[...] = jnp.exp(own - top) / total
-    post(0, 48)
     ring_finish(2)
-    attend(0)
-    partial_start(0)
+    attend(0, 0)
+    partial_start(0, 0)
+    stat_finish(1)
+    post(1)
+    partial_cross(0)
+    attend(0, 1)
+    partial_start(0, 1)
     ring_finish(3)
-    partial_cross(0)
-    attend(1)
-    partial_start(1)
+    attend(1, 0)
+    partial_start(1, 0)
+    attend(1, 1)
     partial_cross(1)
+    partial_start(1, 1)
     partial_finish(0)
     partial_finish(1)
     for c in sends:
@@ -332,12 +392,6 @@
 
 
 def local(activations, w_query, w_key, w_value, pre_mix, post_mix, span_place):
-    ctx = lax.axis_index("ctx")
-    xh, y, core = ctx // 8, (ctx // 2) % 4, ctx % 2
-    positions = (span_place[:, None] * SPAN + jnp.arange(SPAN, dtype=jnp.int32)[None, :]).reshape(2, 4, 2, ROWS)
-    query_pos = lax.dynamic_index_in_dim(positions, y, 1, keepdims=False).reshape(TILE, 1)
-    key_pos = lax.dynamic_index_in_dim(positions, xh, 0, keepdims=False)
-    key_pos = lax.dynamic_index_in_dim(key_pos, core, 1, keepdims=False).reshape(1, TILE)
     any_spec = pl.BlockSpec(memory_space=pl.ANY)
     vmem = pl.BlockSpec(memory_space=pltpu.VMEM)
     dma = pltpu.SemaphoreType.DMA
@@ -345,7 +399,7 @@
         kernel,
         name="heads",
         out_shape=jax.ShapeDtypeStruct((ROWS, MODEL), BF16),
-        in_specs=[any_spec] * 4 + [vmem] * 4,
+        in_specs=[any_spec] * 4 + [vmem] * 2 + [pl.BlockSpec(memory_space=pltpu.SMEM)],
         out_specs=vmem,
         scratch_shapes=[
             pltpu.VMEM((ROWS, SEQS, MODEL), BF16),
@@ -356,8 +410,9 @@
             pltpu.VMEM((2, 4, ROWS, HALF), BF16),
             pltpu.VMEM((2, 4, ROWS, HALF), BF16),
             pltpu.VMEM((HEADS, TILE, TILE), F32),
-            pltpu.VMEM((MIX, 128), F32),
-            pltpu.VMEM((3, MIX, 128), F32),
+            pltpu.VMEM((2, MIX, 128), F32),
+            pltpu.VMEM((2, 3, MIX, 128), F32),
+            pltpu.VMEM((SLAB, TILE), jnp.int32),
             pltpu.VMEM((2, 4, ROWS, HALF), BF16),
             pltpu.VMEM((2, 3, ROWS, HALF), BF16),
             pltpu.VMEM((MIX, MIX), BF16),
@@ -368,14 +423,14 @@
             dma((6, 7)), dma((6, 7)),
             dma((4, 4)), dma((4, 4)),
             dma((2, 3)), dma((2, 3)),
-            dma((3,)), dma((3,)),
+            dma((2, 3)), dma((2, 3)),
             dma((2, 3)), dma((2, 3)),
         ],
         compiler_params=pltpu.CompilerParams(
             collective_id=0, has_side_effects=True, vmem_limit_bytes=60 * 2**20
         ),
         cost_estimate=pl.CostEstimate(flops=30 * 10**9, bytes_accessed=30 * 10**6, transcendentals=5 * 10**6),
-    )(activations, w_query, w_key, w_value, pre_mix, post_mix, query_pos, key_pos)
+    )(activations, w_query, w_key, w_value, pre_mix, post_mix, span_place)
     return out.reshape(ROWS, 1, MODEL)
 
 

time: 147 us -> 113 us (0.77)
  Pallas kernels: 142 us -> 111 us
  local copies, waits for them, and re-layouts: 3.96 us -> 2.06 us
    pallas_call x1, Pallas kernels: 142 us -> 111 us  [local(): pl.pallas_call(kernel, name='heads', out_shape=jax.ShapeDtypeStruct((ROWS...]
    reshape x2 -> x0, local copies, waits for them, and re-layouts: 1.51 us -> none  [the longest x1 0.85 us: local(): lax.dynamic_index_in_dim(positions, y, 1, keepdims=False).reshape(TILE, 1)]
where the time goes in v1:
time: 113 us
  Pallas kernels  111 us (98%)
  local copies, waits for them, and re-layouts  2.06 us (2%)
    pallas_call x1, Pallas kernels, local(): pl.pallas_call(kernel, name='heads', out_shape=jax.ShapeDtypeStruct((ROWS...  111 us

profile of v1, /device:TPU:1, one launch (start us, length us, event | category | flops | bytes accessed | tf_op | source)
XLA Modules:
  0.0 112.8 jit_solution(10032356587190371182)
XLA Ops:
  0.0 110.8 %heads.1 = bf16[96,4096]{1,0:T(8,128)(2,1)} custom-call(bf16[96,8,4096]{2,1,0:T(8,128)(2,1)} %act.1, bf16[4096,512]{1,0:T(8,128)(2,1)} %w_query.1, bf16[4096,512]{1,0:T(8,128)(2,1)} %w_key.1, bf16[4096,512]{1,0:T(8,128)(2,1)} %w_value.1, f32[32,32]{1,0:T(8,128)} %pre_mix.1, f32[32,32]{1,0:T(8,128)} %post_mix.1, s32[32]{0:T(128)} %span_place.1), custom_call_target="tpu_custom_call" | custom-call | flops 30000001024 | bytes 30000000 | tf_op jit(solution)/shard_map/heads/pallas_call | solution.py:398
  110.8 2.1 %copy.9 = bf16[96,1,4096]{2,0,1:T(8,128)(2,1)} copy(bf16[96,1,4096]{2,0,1:T(8,128)(2,1)} %bitcast.1) | data formatting | bytes 1572864

commit v2 on v1

v2 whole, which is shorter than its diff:
```python
import functools

import jax
import jax.numpy as jnp
from jax import lax
from jax.experimental import pallas as pl
from jax.experimental.pallas import tpu as pltpu
from jax.sharding import PartitionSpec as P

HEADS = 32
HD = 128
SPAN = 48
MODEL = 4096
SEQS = 8
ROWS = 96
TILE = 384
SLAB = 8
SLABS = TILE // SLAB
MIX = HEADS * SLAB
WIDE = 256
PARTS = 4
PART = MODEL // PARTS
FLOOR = -1e30
GROUPS = 3
GROUP_ROWS = ROWS // GROUPS
GROUP_SLABS = SLABS // GROUPS
MESH = pl.DeviceIdType.MESH
F32 = jnp.float32
BF16 = jnp.bfloat16

QUERY, KEY, VALUE = 0, 1, 2

CHUNKS = ((KEY, 0), (KEY, 1), (QUERY, 0), (QUERY, 1), (VALUE, 0), (VALUE, 1))

MOVES = (
    (KEY, 0, 0, 32), (KEY, 0, 32, 32), (KEY, 0, 64, 32), (KEY, 1, 0, 96),
    (VALUE, 0, 0, 96), (VALUE, 1, 0, 96), (VALUE, 2, 0, 96), (VALUE, 3, 0, 96),
    (QUERY, 0, 0, 96), (QUERY, 1, 0, 96),
)


def dot(a, b):
    return jnp.dot(a, b, preferred_element_type=F32)


def split(x):
    high = x.astype(BF16)
    return high, (x - high.astype(F32)).astype(BF16)


def spread_mix(mix, high_ref, low_ref):
    row = lax.broadcasted_iota(jnp.int32, (MIX, HEADS), 0) // SLAB
    col = lax.broadcasted_iota(jnp.int32, (MIX, HEADS), 1)
    pick = jnp.where(row == col, 1.0, 0.0).astype(BF16)
    same = (lax.broadcasted_iota(jnp.int32, (MIX, MIX), 0) % SLAB) == (
        lax.broadcasted_iota(jnp.int32, (MIX, MIX), 1) % SLAB
    )
    for part, ref in zip(split(mix), (high_ref, low_ref)):
        tall = dot(pick, part).astype(BF16)
        full = lax.dot_general(tall, pick, (((1,), (1,)), ((), ())), preferred_element_type=F32)
        ref[...] = jnp.where(same, full, 0.0).astype(BF16)


def kernel(
    act, w_query, w_key, w_value, pre_mix, post_mix, span_place, out,
    act_v, w_v, res, stage, stage_v, q_buf, k_buf, v_buf, scores, stat, stat_out, stat_in, key_pos, logits_even, logits_odd,
    part, part_in, pre_high, pre_low, post_high, post_low,
    act_sem, w_sem, own_sem, a2a_send, a2a_recv, y_send, y_recv, q_send, q_recv,
    stat_send, stat_recv, p_send, p_recv,
):
    ctx, tp = lax.axis_index("ctx"), lax.axis_index("tp")
    xh, y, core = ctx // 8, (ctx // 2) % 4, ctx % 2
    up = (xh * 8 + ((y + 1) % 4) * 2 + core, tp)
    down = (xh * 8 + ((y + 3) % 4) * 2 + core, tp)
    y_up, y_down = (y + 1) % 4, (y + 3) % 4
    sibling = (ctx + 1 - 2 * core, tp)
    partner = ((1 - xh) * 8 + y * 2 + core, tp)
    diagonal = ((1 - xh) * 8 + y * 2 + 1 - core, tp)
    mine = xh * 2 + core
    sibling_slot = xh * 2 + 1 - core
    partner_slot = (1 - xh) * 2 + core
    diagonal_slot = (1 - xh) * 2 + 1 - core
    peers = [(ctx, (tp + o) % SEQS) for o in range(1, SEQS)]

    weights = (w_query, w_key, w_value)
    buffers = (q_buf, k_buf, v_buf)

    act_copies = []
    for b in range(3):
        rows = pl.ds(b * 32, 32)
        act_copies.append(pltpu.make_async_copy(act.at[rows], act_v.at[rows], act_sem.at[b]))
    w_copies = []
    for n, (kind, j) in enumerate(CHUNKS):
        w_copies.append(
            pltpu.make_async_copy(weights[kind].at[:, pl.ds(j * WIDE, WIDE)], w_v.at[n % 3], w_sem.at[n])
        )
    w_copies[0].start()
    for c in act_copies:
        c.start()

    barrier = pltpu.get_barrier_semaphore()
    friends = peers + [up, down, sibling, partner, diagonal]
    for friend in friends:
        pl.semaphore_signal(barrier, inc=1, device_id=friend, device_id_type=MESH)

    spread_mix(pre_mix[...] * (HD ** -0.5), pre_high, pre_low)
    spread_mix(post_mix[...], post_high, post_low)
    stat[...] = jnp.zeros_like(stat)
    column = lax.broadcasted_iota(jnp.int32, (SLAB, TILE), 1)
    position = column % SPAN
    for n in range(TILE // SPAN):
        place = span_place[(xh * 8 + (n // 2) * 2 + core) * 2 + n % 2]
        position = jnp.where(column // SPAN == n, position + place * SPAN, position)
    key_pos[...] = position

    sends = []

    def remote(src, dst, send, recv, to):
        copy = pltpu.make_async_remote_copy(
            src_ref=src, dst_ref=dst, send_sem=send, recv_sem=recv, device_id=to, device_id_type=MESH
        )
        sends.append(copy)
        return copy

    def slot_of(kind):
        return mine if kind == 0 else y

    exchange = {}

    def project(n):
        kind, j = CHUNKS[n]
        w_copies[n].wait()
        for b in range(3):
            if n == 0:
                act_copies[b].wait()
                if b == 2:
                    w_copies[1].start()
                    w_copies[2].start()
            rows = act_v[b * 32:(b + 1) * 32].reshape(32 * SEQS, MODEL)
            both = dot(rows, w_v[n % 3])
            for i in range(2):
                res[i] = both[:, i * HD:(i + 1) * HD]
            for s in range(SEQS):
                for i in range(2):
                    block = res[i, pl.ds(s, 32, stride=SEQS), :].astype(BF16)
                    if kind == VALUE:
                        stage_v[2 * j + i, s, b * 32:(b + 1) * 32, :] = block
                    else:
                        stage[kind, j, s, b * 32:(b + 1) * 32, i * HD:(i + 1) * HD] = block
            if n == 0:
                if b == 0:
                    pl.semaphore_wait(barrier, len(friends))
                scatter(b)
        if n > 0 and n + 2 < len(CHUNKS):
            w_copies[n + 2].start()

    def scatter(e):
        kind, j, row, rows = MOVES[e]
        source, width = (stage_v.at[j], HD) if kind == VALUE else (stage.at[kind, j], WIDE)
        rows = pl.ds(row, rows)
        here = buffers[kind].at[j, slot_of(kind), rows, pl.ds(pl.multiple_of(tp * width, width), width)]
        copies = []
        for o, peer in enumerate(peers):
            copies.append(
                remote(source.at[peer[1], rows], here, a2a_send.at[e, o], a2a_recv.at[e, o], peer)
            )
            copies[-1].start()
        own = pltpu.make_async_copy(source.at[tp, rows], here, own_sem.at[e])
        own.start()
        exchange[e] = (copies, own)

    def arrived(e):
        copies, own = exchange[e]
        own.wait()
        for c in copies:
            c.wait_recv()

    ring = {}

    def ring_start(e):
        kind, j, row, rows = MOVES[e]
        arrived(e)
        block = buffers[kind].at[j, y, pl.ds(row, rows)]
        copies = []
        for m, to in enumerate((up, down)):
            copies.append(remote(block, block, y_send.at[e, m], y_recv.at[e, m], to))
            copies[-1].start()
        ring[e] = copies

    def ring_forward(e):
        kind, j, row, rows = MOVES[e]
        copies = ring[e]
        for m, (source, to) in enumerate(((y_down, up), (y_up, down))):
            copies[m].wait_recv()
            block = buffers[kind].at[j, source, pl.ds(row + m * (rows // 2), rows // 2)]
            copies[m] = remote(block, block, y_send.at[e, 2 + m], y_recv.at[e, 2 + m], to)
            copies[m].start()

    def ring_finish(e):
        for c in ring[e]:
            c.wait_recv()

    queries = {}

    def query_start(j):
        arrived(8 + j)
        a = remote(q_buf.at[j, mine], q_buf.at[j, mine], q_send.at[j, 1], q_recv.at[j, 1], partner)
        b = remote(q_buf.at[j, mine], q_buf.at[j, mine], q_send.at[j, 0], q_recv.at[j, 0], sibling)
        a.start()
        b.start()
        queries[j] = [a, b]

    def query_forward(j):
        a, b = queries[j]
        a.wait_recv()
        there = q_buf.at[j, partner_slot]
        c = remote(there, there, q_send.at[j, 2], q_recv.at[j, 2], sibling)
        c.start()
        queries[j] = [b, c]

    def query_finish(j):
        for c in queries[j]:
            c.wait_recv()

    def score(j):
        def one(g, carry):
            for u in range(4):
                hh = g * 4 + u
                lanes = pl.ds(pl.multiple_of(hh * HD, HD), HD)
                q = q_buf[j, :, :, lanes].reshape(TILE, HD)
                k = k_buf[j, :, :, lanes].reshape(TILE, HD)
                scores[(hh // 2) * PARTS + 2 * j + hh % 2] = lax.dot_general(
                    q, k, (((1,), (1,)), ((), ())), preferred_element_type=F32
                )
            return carry

        lax.fori_loop(0, HEADS // 8, one, 0)

    lane = lax.broadcasted_iota(jnp.int32, (MIX, 128), 1)
    minor = lax.broadcasted_iota(jnp.int32, (SLAB, 1), 0)
    per_slot = GROUP_ROWS // SLAB

    logits_of = (logits_even, logits_odd)

    def slab_rows(step, u):
        group, slot = divmod(step, 4)
        first = slot * ROWS + group * GROUP_ROWS + u * SLAB
        return slice(first, first + SLAB)

    def premix(step):
        x = jnp.concatenate(
            [scores[:, slab_rows(step, u), :].reshape(MIX, TILE) for u in range(per_slot)], axis=1
        )
        high, low = split(x)
        logits_of[step % 2][...] = dot(pre_high[...], high) + dot(pre_low[...], high) + dot(pre_high[...], low)

    def softmax_step(step):
        group, slot = divmod(step, 4)
        stats = stat[group]
        for u in range(per_slot):
            i = slot * per_slot + u
            inside = group * GROUP_ROWS + u * SLAB
            span = ((slot // 2) * 8 + y * 2 + slot % 2) * 2 + inside // SPAN
            seen = key_pos[...] <= span_place[span] * SPAN + inside % SPAN + minor
            logits = logits_of[step % 2][:, u * TILE:(u + 1) * TILE].reshape(HEADS, SLAB, TILE)
            masked = jnp.where(seen[None], logits, FLOOR).reshape(MIX, TILE)
            top = jnp.max(masked, axis=1, keepdims=True)
            e = jnp.exp(masked - top)
            total = jnp.sum(e, axis=1, keepdims=True)
            scores[:, slab_rows(step, u), :] = e.reshape(HEADS, SLAB, TILE)
            stats = jnp.where(lane == i, top, jnp.where(lane == i + GROUP_SLABS, total, stats))
        stat[group] = stats

    def softmax(first, last):
        if first == 0:
            premix(0)
        for step in range(first, last):
            if step + 1 < 4 * GROUPS:
                premix(step + 1)
            softmax_step(step)

    stat_copies = {}

    def stat_start(group):
        packed = stat[group, 0:64, :]
        for q in range(1, 4):
            packed += pltpu.roll(stat[group, q * 64:(q + 1) * 64, :], q * 32, 1)
        stat_out[group] = packed
        copies = []
        for n, to in enumerate((sibling, partner, diagonal)):
            copies.append(
                remote(
                    stat_out.at[group], stat_in.at[group, n],
                    stat_send.at[group, n], stat_recv.at[group, n], to,
                )
            )
            copies[-1].start()
        stat_copies[group] = copies

    def stat_finish(group):
        for c in stat_copies[group]:
            c.wait_recv()
        own = stat_out[group]
        others = [stat_in[group, n] for n in range(3)]
        top = functools.reduce(jnp.maximum, others, own)
        total = sum(jnp.exp(s - top) * pltpu.roll(s, 128 - GROUP_SLABS, 1) for s in [own] + others)
        weights = jnp.exp(own - top) / total
        stat[group, 0:64, :] = weights
        for q in range(1, 4):
            stat[group, q * 64:(q + 1) * 64, :] = pltpu.roll(weights, 128 - q * 32, 1)

    far, near = 1 - xh, xh

    def post(group, pair):
        slabs = [pair * 2 * per_slot + u for u in range(2 * per_slot)]
        rows = [
            pl.ds(
                pl.multiple_of(
                    (pair * 2 + u // per_slot) * ROWS + group * GROUP_ROWS + (u % per_slot) * SLAB, SLAB
                ),
                SLAB,
            )
            for u in range(2 * per_slot)
        ]
        weights = stat[group]
        probs = []
        for i, r in zip(slabs, rows):
            weight = jnp.sum(jnp.where(lane == i, weights, 0.0), axis=1, keepdims=True)
            probs.append((scores[:, r, :].reshape(MIX, TILE) * weight).astype(BF16))
        probs = jnp.concatenate(probs, axis=1)
        mixed = dot(post_high[...], probs) + dot(post_low[...], probs)
        for u, r in enumerate(rows):
            scores[:, r, :] = mixed[:, u * TILE:(u + 1) * TILE].reshape(HEADS, SLAB, TILE)

    def attend(j, pair):
        rows = pl.ds(pl.multiple_of(pair * 2 * ROWS, 2 * ROWS), 2 * ROWS)

        def one(g, carry):
            for u in range(4):
                t = g * 4 + u
                lanes = pl.ds(pl.multiple_of(t * HD, HD), HD)
                v = v_buf[j, :, :, lanes].reshape(TILE, HD)
                m = scores[t * PARTS + j, rows, :].astype(BF16)
                part[j, pl.ds(pair * 2, 2), :, lanes] = dot(m, v).reshape(2, ROWS, HD).astype(BF16)
            return carry

        lax.fori_loop(0, SEQS // 4, one, 0)

    partial = {}

    def partial_start(j, n):
        slot = (diagonal_slot, sibling_slot)[n]
        partial[j, n] = remote(part.at[j, slot], part_in.at[j, n], p_send.at[j, n], p_recv.at[j, n], sibling)
        partial[j, n].start()

    def attend_far(j):
        attend(j, far)
        partial_start(j, 0)

    def attend_near(j):
        attend(j, near)
        partial_start(j, 1)

    def partial_cross(j):
        partial[j, 0].wait_recv()
        both = part.at[j, partner_slot]
        both[...] = (both[...].astype(F32) + part_in[j, 0].astype(F32)).astype(BF16)
        partial[j, 2] = remote(both, part_in.at[j, 2], p_send.at[j, 2], p_recv.at[j, 2], partner)
        partial[j, 2].start()

    def partial_finish(j):
        partial[j, 1].wait_recv()
        partial[j, 2].wait_recv()
        done = (
            part[j, mine].astype(F32) + part_in[j, 1].astype(F32) + part_in[j, 2].astype(F32)
        ).astype(BF16)
        for t in range(SEQS):
            head = t * PARTS + j
            out[:, head * HD:(head + 1) * HD] = done[:, t * HD:(t + 1) * HD]

    project(0)
    project(1)
    ring_start(0)
    scatter(3)
    project(2)
    scatter(8)
    ring_start(1)
    ring_start(2)
    project(3)
    scatter(9)
    ring_forward(0)
    ring_forward(1)
    project(4)
    ring_start(3)
    ring_forward(2)
    scatter(4)
    scatter(5)
    project(5)
    scatter(6)
    scatter(7)
    query_start(0)
    query_start(1)
    ring_forward(3)
    ring_start(4)
    query_forward(0)
    ring_start(5)
    ring_finish(0)
    ring_finish(1)
    ring_finish(2)
    query_finish(0)
    score(0)
    query_forward(1)
    ring_finish(3)
    query_finish(1)
    score(1)
    softmax(0, 2)
    ring_start(6)
    ring_start(7)
    softmax(2, 4)
    stat_start(0)
    ring_forward(4)
    softmax(4, 8)
    stat_start(1)
    ring_forward(5)
    softmax(8, 12)
    stat_start(2)
    stat_finish(0)
    post(0, far)
    stat_finish(1)
    post(1, far)
    ring_forward(6)
    stat_finish(2)
    post(2, far)
    ring_finish(4)
    attend_far(0)
    ring_finish(5)
    attend_far(1)
    partial_cross(0)
    ring_forward(7)
    post(0, near)
    partial_cross(1)
    ring_finish(6)
    attend_far(2)
    post(1, near)
    partial_cross(2)
    post(2, near)
    ring_finish(7)
    attend_far(3)
    attend_near(0)
    partial_cross(3)
    attend_near(1)
    attend_near(2)
    attend_near(3)
    partial_finish(0)
    partial_finish(1)
    partial_finish(2)
    partial_finish(3)
    for c in sends:
        c.wait_send()


def local(activations, w_query, w_key, w_value, pre_mix, post_mix, span_place):
    any_spec = pl.BlockSpec(memory_space=pl.ANY)
    vmem = pl.BlockSpec(memory_space=pltpu.VMEM)
    dma = pltpu.SemaphoreType.DMA
    out = pl.pallas_call(
        kernel,
        name="heads",
        out_shape=jax.ShapeDtypeStruct((ROWS, MODEL), BF16),
        in_specs=[any_spec] * 4 + [vmem] * 2 + [pl.BlockSpec(memory_space=pltpu.SMEM)],
        out_specs=vmem,
        scratch_shapes=[
            pltpu.VMEM((ROWS, SEQS, MODEL), BF16),
            pltpu.VMEM((3, MODEL, WIDE), BF16),
            pltpu.VMEM((2, 256, HD), F32),
            pltpu.VMEM((2, 2, SEQS, ROWS, WIDE), BF16),
            pltpu.VMEM((PARTS, SEQS, ROWS, HD), BF16),
            pltpu.VMEM((2, 4, ROWS, 2 * PART), BF16),
            pltpu.VMEM((2, 4, ROWS, 2 * PART), BF16),
            pltpu.VMEM((PARTS, 4, ROWS, PART), BF16),
            pltpu.VMEM((HEADS, TILE, TILE), F32),
            pltpu.VMEM((GROUPS, MIX, 128), F32),
            pltpu.VMEM((GROUPS, MIX // 4, 128), F32),
            pltpu.VMEM((GROUPS, 3, MIX // 4, 128), F32),
            pltpu.VMEM((SLAB, TILE), jnp.int32),
            pltpu.VMEM((MIX, GROUP_SLABS // 4 * TILE), F32),
            pltpu.VMEM((MIX, GROUP_SLABS // 4 * TILE), F32),
            pltpu.VMEM((PARTS, 4, ROWS, PART), BF16),
            pltpu.VMEM((PARTS, 3, ROWS, PART), BF16),
            pltpu.VMEM((MIX, MIX), BF16),
            pltpu.VMEM((MIX, MIX), BF16),
            pltpu.VMEM((MIX, MIX), BF16),
            pltpu.VMEM((MIX, MIX), BF16),
            dma((3,)), dma((len(CHUNKS),)), dma((len(MOVES),)),
            dma((len(MOVES), SEQS - 1)), dma((len(MOVES), SEQS - 1)),
            dma((len(MOVES) - 2, 4)), dma((len(MOVES) - 2, 4)),
            dma((2, 3)), dma((2, 3)),
            dma((GROUPS, 3)), dma((GROUPS, 3)),
            dma((PARTS, 3)), dma((PARTS, 3)),
        ],
        compiler_params=pltpu.CompilerParams(
            collective_id=0, has_side_effects=True, vmem_limit_bytes=60 * 2**20
        ),
        cost_estimate=pl.CostEstimate(flops=30 * 10**9, bytes_accessed=30 * 10**6, transcendentals=5 * 10**6),
    )(activations, w_query, w_key, w_value, pre_mix, post_mix, span_place)
    return out.reshape(ROWS, 1, MODEL)


def solution(mesh):
    placed = (P("ctx", None, None), P(None, "tp"), P(None, "tp"), P(None, "tp"), P(), P(), P())
    return jax.shard_map(
        local, mesh=mesh, in_specs=placed, out_specs=P("ctx", "tp", None), check_vma=False
    )
```

time: 113 us -> 101 us (0.89)
  Pallas kernels: 111 us -> 98.6 us
    pallas_call x1, Pallas kernels: 111 us -> 98.6 us  [local(): pl.pallas_call(kernel, name='heads', out_shape=jax.ShapeDtypeStruct((ROWS...]
where the time goes in v2:
time: 101 us
  Pallas kernels  98.6 us (98%)
  local copies, waits for them, and re-layouts  2.06 us (2%)
    pallas_call x1, Pallas kernels, local(): pl.pallas_call(kernel, name='heads', out_shape=jax.ShapeDtypeStruct((ROWS...  98.6 us
    unnamed x1, local copies, waits for them, and re-layouts  2.06 us

profile of v2, /device:TPU:1, one launch (start us, length us, event | category | flops | bytes accessed | tf_op | source)
XLA Modules:
  0.0 100.7 jit_solution(15202779018920850766)
XLA Ops:
  0.0 98.6 %heads.1 = bf16[96,4096]{1,0:T(8,128)(2,1)} custom-call(bf16[96,8,4096]{2,1,0:T(8,128)(2,1)} %act.1, bf16[4096,512]{1,0:T(8,128)(2,1)} %w_query.1, bf16[4096,512]{1,0:T(8,128)(2,1)} %w_key.1, bf16[4096,512]{1,0:T(8,128)(2,1)} %w_value.1, f32[32,32]{1,0:T(8,128)} %pre_mix.1, f32[32,32]{1,0:T(8,128)} %post_mix.1, s32[32]{0:T(128)} %span_place.1), custom_call_target="tpu_custom_call" | custom-call | flops 30000001024 | bytes 30000000 | tf_op jit(solution)/shard_map/heads/pallas_call | solution.py:466
  98.7 2.1 %copy.9 = bf16[96,1,4096]{2,0,1:T(8,128)(2,1)} copy(bf16[96,1,4096]{2,0,1:T(8,128)(2,1)} %bitcast.1) | data formatting | bytes 1572864

commit v3 on v2

--- a/solution.py
+++ b/solution.py
@@ -30,7 +30,7 @@
 
 QUERY, KEY, VALUE = 0, 1, 2
 
-CHUNKS = ((KEY, 0), (KEY, 1), (QUERY, 0), (QUERY, 1), (VALUE, 0), (VALUE, 1))
+CHUNKS = ((KEY, 0), (QUERY, 0), (KEY, 1), (QUERY, 1), (VALUE, 0), (VALUE, 1))
 
 MOVES = (
     (KEY, 0, 0, 32), (KEY, 0, 32, 32), (KEY, 0, 64, 32), (KEY, 1, 0, 96),
@@ -224,8 +224,8 @@
 
     def score(j):
         def one(g, carry):
-            for u in range(4):
-                hh = g * 4 + u
+            for u in range(8):
+                hh = g * 8 + u
                 lanes = pl.ds(pl.multiple_of(hh * HD, HD), HD)
                 q = q_buf[j, :, :, lanes].reshape(TILE, HD)
                 k = k_buf[j, :, :, lanes].reshape(TILE, HD)
@@ -234,7 +234,7 @@
                 )
             return carry
 
-        lax.fori_loop(0, HEADS // 8, one, 0)
+        lax.fori_loop(0, HEADS // 16, one, 0)
 
     lane = lax.broadcasted_iota(jnp.int32, (MIX, 128), 1)
     minor = lax.broadcasted_iota(jnp.int32, (SLAB, 1), 0)
@@ -336,15 +336,15 @@
         rows = pl.ds(pl.multiple_of(pair * 2 * ROWS, 2 * ROWS), 2 * ROWS)
 
         def one(g, carry):
-            for u in range(4):
-                t = g * 4 + u
-                lanes = pl.ds(pl.multiple_of(t * HD, HD), HD)
+            for u in range(8):
+                t = g * 8 + u
+                lanes = slice(t * HD, (t + 1) * HD)
                 v = v_buf[j, :, :, lanes].reshape(TILE, HD)
                 m = scores[t * PARTS + j, rows, :].astype(BF16)
                 part[j, pl.ds(pair * 2, 2), :, lanes] = dot(m, v).reshape(2, ROWS, HD).astype(BF16)
             return carry
 
-        lax.fori_loop(0, SEQS // 4, one, 0)
+        one(0, 0)
 
     partial = {}
 
@@ -381,9 +381,9 @@
     project(0)
     project(1)
     ring_start(0)
+    scatter(8)
+    project(2)
     scatter(3)
-    project(2)
-    scatter(8)
     ring_start(1)
     ring_start(2)
     project(3)
@@ -444,12 +444,12 @@
     post(1, near)
     partial_cross(2)
     post(2, near)
+    attend_near(0)
+    attend_near(1)
     ring_finish(7)
     attend_far(3)
-    attend_near(0)
+    attend_near(2)
     partial_cross(3)
-    attend_near(1)
-    attend_near(2)
     attend_near(3)
     partial_finish(0)
     partial_finish(1)

time: 101 us -> 100 us (0.990)
  no operation moved by 1% of the time
where the time goes in v3:
time: 100 us
  Pallas kernels  98 us (98%)
  local copies, waits for them, and re-layouts  2.06 us (2%)
    pallas_call x1, Pallas kernels, local(): pl.pallas_call(kernel, name='heads', out_shape=jax.ShapeDtypeStruct((ROWS...  98 us
    unnamed x1, local copies, waits for them, and re-layouts  2.06 us

profile of v3, /device:TPU:1, one launch (start us, length us, event | category | flops | bytes accessed | tf_op | source)
XLA Modules:
  0.0 100.0 jit_solution(7477427841918958831)
XLA Ops:
  0.0 98.0 %heads.1 = bf16[96,4096]{1,0:T(8,128)(2,1)} custom-call(bf16[96,8,4096]{2,1,0:T(8,128)(2,1)} %act.1, bf16[4096,512]{1,0:T(8,128)(2,1)} %w_query.1, bf16[4096,512]{1,0:T(8,128)(2,1)} %w_key.1, bf16[4096,512]{1,0:T(8,128)(2,1)} %w_value.1, f32[32,32]{1,0:T(8,128)} %pre_mix.1, f32[32,32]{1,0:T(8,128)} %post_mix.1, s32[32]{0:T(128)} %span_place.1), custom_call_target="tpu_custom_call" | custom-call | flops 30000001024 | bytes 30000000 | tf_op jit(solution)/shard_map/heads/pallas_call | solution.py:466
  98.0 2.1 %copy.9 = bf16[96,1,4096]{2,0,1:T(8,128)(2,1)} copy(bf16[96,1,4096]{2,0,1:T(8,128)(2,1)} %bitcast.1) | data formatting | bytes 1572864
